TPU v7x, 32 devices: a whole 2x2x4 slice. The times are simulated.
32 devices in a mesh: gx: 8 (over z, y), gy: 4 (over x, core).
Axes of the slice: x: 2, y: 2, z: 4, core: 2. Of those that a mesh axis runs over, the one named last changes fastest.
Arguments:
- density: bfloat16 [8, 4, 3, 20, 128, 128], P('gx', 'gy'), may hold values from -0.3 to 0.8
- neighbours: int32 [8, 4, 3, 20], replicated, may hold values from 0 to 95, as said below
- ent_blocks: bfloat16 [768, 128, 128], P(('gx', 'gy')), may hold values from -0.59765625 to 0.59765625
- ent_owner: int32 [768], replicated, may hold values from 0 to 31, as said below
- ent_place: int32 [768], replicated, may hold values from 0 to 59
Outputs:
- purified: float32 [8, 4, 3, 20, 128, 128], P('gx', 'gy')
Inputs may be any that keep to these rules, and one draw needn't show every extreme that they name: neighbours[x, y, r, 0] is the row's own index (x * 4 + y) * 3 + r; the other 19 entries of a row are distinct rows of devices (x + a mod 8, y + b mod 4) with a and b in -1, 0, 1. `ent_owner`: among the 24 entries d * 24 to d * 24 + 23 of one device d, no owner is named more than 2 times, and some owner exactly 2 times.
All inputs are finite; a program needn't handle non-finite values.
Results may differ from a plain program's by a relative error of at most 0.0059.
Values may be sent and summed in bfloat16 or wider, within the bound.
A program may use at most 128 MiB of HBM per device.

v0:
```python
import jax
import jax.numpy as jnp
from jax import lax
from jax.sharding import PartitionSpec as P

C = 2


def with_halo(cells, sides, width):
    for axis, dim in sides:
        count = lax.axis_size(axis)
        head = lax.slice_in_dim(cells, 0, width, axis=dim)
        tail = lax.slice_in_dim(cells, cells.shape[dim] - width, cells.shape[dim], axis=dim)
        cells = jnp.concatenate(
            [
                lax.ppermute(tail, axis, [(i, (i + 1) % count) for i in range(count)]),
                cells,
                lax.ppermute(head, axis, [((i + 1) % count, i) for i in range(count)]),
            ],
            axis=dim,
        )
    return cells


def block_positions(neighbours, here_x, here_y, row_columns):
    wide_count, narrow_count, row_count, slot_count = neighbours.shape
    listing = neighbours.reshape(wide_count * narrow_count * row_count, slot_count)
    inner_lists = jnp.take(listing, row_columns, axis=0)
    matches = inner_lists[:, None, :] == row_columns[None, :, None]
    present = jnp.any(matches, axis=2)
    slot_ids = jnp.arange(slot_count, dtype=jnp.int32)
    inner_slot = jnp.sum(jnp.where(matches, slot_ids[None, None, :], 0), axis=2)
    inner_x = row_columns // (narrow_count * row_count)
    inner_y = row_columns // row_count % narrow_count
    inner_r = row_columns % row_count
    near_x = (inner_x - here_x + 1) % wide_count
    near_y = (inner_y - here_y + 1) % narrow_count
    near_row = (near_x * 3 + near_y) * row_count + inner_r
    position = near_row[:, None] * slot_count + inner_slot
    return jnp.where(present, position, 9 * row_count * slot_count)


def per_device(density, neighbours, ent_blocks, ent_owner, ent_place):
    wide_count = lax.axis_size("gx")
    narrow_count = lax.axis_size("gy")
    device_count = wide_count * narrow_count
    here_x = lax.axis_index("gx")
    here_y = lax.axis_index("gy")
    self_index = here_x * narrow_count + here_y
    row_count = density.shape[2]
    slot_count = density.shape[3]
    width = density.shape[4]
    area = width * width
    arrivals_held = ent_blocks.shape[0]
    owners = ent_owner.reshape(device_count, arrivals_held)
    places = ent_place.reshape(device_count, arrivals_held)
    entry_ids = jnp.arange(arrivals_held, dtype=jnp.int32)
    same_owner = owners[:, :, None] == owners[:, None, :]
    earlier = entry_ids[None, None, :] < entry_ids[None, :, None]
    ranks = jnp.sum(same_owner & earlier, axis=2)
    my_owners = lax.dynamic_index_in_dim(owners, self_index, 0, False)
    my_ranks = lax.dynamic_index_in_dim(ranks, self_index, 0, False)
    send_slot = my_owners * C + my_ranks
    buffer_ids = jnp.arange(device_count * C, dtype=jnp.int32)
    send_map = (buffer_ids[:, None] == send_slot[None, :]).astype(jnp.bfloat16)
    outgoing = jnp.dot(
        send_map, ent_blocks.reshape(arrivals_held, area), preferred_element_type=jnp.float32
    ).astype(jnp.bfloat16)
    received = lax.all_to_all(outgoing, ("gx", "gy"), split_axis=0, concat_axis=0, tiled=True)
    for_me = owners == self_index
    capacity_ids = jnp.arange(C, dtype=jnp.int32)
    picked = for_me[:, :, None] & (ranks[:, :, None] == capacity_ids[None, None, :])
    slot_place = jnp.sum(jnp.where(picked, places[:, :, None], 0), axis=1)
    slot_used = jnp.any(picked, axis=1)
    target_ids = jnp.arange(row_count * slot_count, dtype=jnp.int32)
    receive_map = (
        (target_ids[:, None] == slot_place.reshape(1, -1)) & slot_used.reshape(1, -1)
    ).astype(jnp.bfloat16)
    increment = jnp.dot(receive_map, received, preferred_element_type=jnp.float32)
    admitted = (
        density.reshape(row_count * slot_count, area).astype(jnp.float32) + increment
    ).astype(jnp.bfloat16)
    admitted = admitted.reshape(density.shape)
    surround = with_halo(admitted, (("gx", 0), ("gy", 1)), 1)
    table = surround.reshape(9 * row_count * slot_count, width, width)
    my_columns = lax.dynamic_index_in_dim(
        lax.dynamic_index_in_dim(neighbours, here_x, 0, False), here_y, 0, False
    )

    def purify_row(item):
        left_blocks, row_columns = item
        position = block_positions(neighbours, here_x, here_y, row_columns)
        gathered = jnp.take(table, position.reshape(-1), axis=0, mode="fill", fill_value=0)
        gathered = gathered.reshape(slot_count, slot_count, width, width)
        square = jnp.einsum(
            "mab,mkbc->kac", left_blocks, gathered, preferred_element_type=jnp.float32
        )
        cube = jnp.einsum(
            "mab,mkbc->kac",
            square.astype(jnp.bfloat16),
            gathered,
            preferred_element_type=jnp.float32,
        )
        return 3.0 * square - 2.0 * cube

    purified = lax.map(purify_row, (admitted[0, 0], my_columns))
    return purified.reshape(density.shape)


def solution(mesh):
    in_specs = (P("gx", "gy", None, None, None, None), P(), P(("gx", "gy"), None, None), P(), P())
    out_specs = P("gx", "gy", None, None, None, None)
    return jax.shard_map(
        per_device, mesh=mesh, in_specs=in_specs, out_specs=out_specs, check_vma=False
    )
```

profile of v0, /device:TPU:0, one launch (start us, length us, event | category | flops | bytes accessed | tf_op | source)
XLA Modules:
  0.0 462.3 jit_solution(4139312476334070661)
XLA Ops:
  3.2 2.6 all_to_all.8
  5.8 7.4 %all-to-all-start = ((bf16[32,2,16384]{2,1,0:T(2,128)(2,1)}), bf16[32,2,16384]{2,1,0:T(2,128)(2,1)}, u32[]{:S(2)}, u32[]{:S(2)}) async-start(bf16[32,2,16384]{2,1,0:T(2,128)(2,1)} %all_to_all.8), calls=%async_computation | async-start | bytes 4194304 | tf_op jit(solution)/shard_map/all_to_all | solution.py:69
  14.5 4.3 copy.46
  18.8 43.3 %all-to-all-done = bf16[32,2,16384]{2,1,0:T(2,128)(2,1)} async-done(((bf16[32,2,16384]{2,1,0:T(2,128)(2,1)}), bf16[32,2,16384]{2,1,0:T(2,128)(2,1)}, u32[]{:S(2)}, u32[]{:S(2)}) %all-to-all-start) | async-done | bytes 2097184 | tf_op jit(solution)/shard_map/all_to_all | solution.py:69
  62.1 2.7 all_to_all.10
  64.8 2.9 fusion.28
  71.0 3.4 collective-permute-start.1
  74.4 80.9 %collective-permute-done = bf16[1,1,3,20,128,128]{5,4,3,2,1,0:T(8,128)(2,1)S(1)} collective-permute-done((bf16[1,1,3,20,128,128]{5,4,3,2,1,0:T(8,128)(2,1)}, bf16[1,1,3,20,128,128]{5,4,3,2,1,0:T(8,128)(2,1)S(1)}, u32[]{:S(2)}, u32[]{:S(2)}) %collective-permute-start) | collective-permute-done | bytes 1966112 | tf_op jit(solution)/shard_map/ppermute | solution.py:16
  156.8 3.0 constant_dynamic-update-slice_fusion.2
  163.1 126.0 %collective-permute-done.2 = bf16[3,1,3,20,128,128]{5,4,3,2,1,0:T(8,128)(2,1)} collective-permute-done((bf16[3,1,3,20,128,128]{5,4,3,2,1,0:T(8,128)(2,1)}, bf16[3,1,3,20,128,128]{5,4,3,2,1,0:T(8,128)(2,1)}, u32[]{:S(2)}, u32[]{:S(2)}) %collective-permute-start.2) | collective-permute-done | bytes 5898272 | tf_op jit(solution)/shard_map/ppermute | solution.py:16
  289.9 15.8 %pad_maximum_fusion = bf16[3,3,3,20,128,128]{5,4,3,2,1,0:T(8,128)(2,1)} fusion(bf16[3,1,3,20,128,128]{5,4,3,2,1,0:T(8,128)(2,1)} %collective-permute-done.3, bf16[3,1,3,20,128,128]{5,4,3,2,1,0:T(8,128)(2,1)} %constant_dynamic-update-slice_fusion.1, bf16[3,1,3,20,128,128]{5,4,3,2,1,0:T(8,128)(2,1)} %collective-permute-done.2), kind=kLoop, calls=%fused_computation.60 | loop fusion | flops 17694720 | bytes 35389440 | tf_op jit(solution)/shard_map/concatenate | solution.py:14
  305.8 156.5 %while.14 = (s32[]{:T(128)}, f32[3,20,128,128]{3,2,1,0:T(8,128)}, s32[3,20]{1,0:T(4,128)S(1)}, s32[8,4,3,20]{3,2,1,0:T(4,128)}, s32[]{:T(128)}, /*index=5*/s32[]...) while((s32[]{:T(128)}, f32[3,20,128,128]{3,2,1,0:T(8,128)}, ...), condition=%wide.wide.region_6.7_spmd, body=%wide.wide.region_3.6_spmd.sunk | while | flops 3369908736 | bytes 140939488 | solution.py:106
  307.7 18.5 %gather_fusion.1 = bf16[400,128,128]{2,1,0:T(8,128)(2,1)} fusion(bf16[540,128,128]{2,1,0:T(8,128)(2,1)} %get-tuple-element.328, s32[1024]{0:T(1024)S(1)} %pad_clamp_fusion.7), kind=kCustom, calls=%fused_computation.1.clone.clone.1 | custom fusion | bytes 26216000 | tf_op jit(solution)/shard_map/while/body/eval_jaxpr/jit(_take)/gather | solution.py:93
  326.2 17.7 %copy.62 = bf16[20,20,128,128]{2,3,0,1:T(8,128)(2,1)} copy(bf16[20,20,128,128]{3,2,1,0:T(8,128)(2,1)} %bitcast.84) | data formatting | bytes 26214400 | tf_op jit(solution)/shard_map/while/body/eval_jaxpr/jit(_take)/gather | solution.py:93
  344.0 8.4 %fusion.59 = f32[20,128,128]{2,1,0:T(8,128)S(1)} fusion(bf16[20,20,128,128]{2,3,0,1:T(8,128)(2,1)} %copy.62, pred[20,20]{0,1:T(8,128)(4,1)S(1)} %copy.63, bf16[3,20,128,128]{3,2,1,0:T(8,128)(2,1)} %get-tuple-element.329, s32[]{:T(128)} %get-tuple-element.312), kind=kOutput, calls=%fused_computation.7.clone.clone.1 | convolution fusion | flops 1684275200 | bytes 15074192 | tf_op jit(solution)/shard_map/while/body/eval_jaxpr/mab,mkbc->kac/dot_general | solution.py:95
  352.6 3.7 fusion.60
  359.8 18.6 %gather_fusion.1 = bf16[400,128,128]{2,1,0:T(8,128)(2,1)} fusion(bf16[540,128,128]{2,1,0:T(8,128)(2,1)} %get-tuple-element.328, s32[1024]{0:T(1024)S(1)} %pad_clamp_fusion.7), kind=kCustom, calls=%fused_computation.1.clone.clone.1 | custom fusion | bytes 26216000 | tf_op jit(solution)/shard_map/while/body/eval_jaxpr/jit(_take)/gather | solution.py:93
  378.4 17.7 %copy.62 = bf16[20,20,128,128]{2,3,0,1:T(8,128)(2,1)} copy(bf16[20,20,128,128]{3,2,1,0:T(8,128)(2,1)} %bitcast.84) | data formatting | bytes 26214400 | tf_op jit(solution)/shard_map/while/body/eval_jaxpr/jit(_take)/gather | solution.py:93
  396.2 8.4 %fusion.59 = f32[20,128,128]{2,1,0:T(8,128)S(1)} fusion(bf16[20,20,128,128]{2,3,0,1:T(8,128)(2,1)} %copy.62, pred[20,20]{0,1:T(8,128)(4,1)S(1)} %copy.63, bf16[3,20,128,128]{3,2,1,0:T(8,128)(2,1)} %get-tuple-element.329, s32[]{:T(128)} %get-tuple-element.312), kind=kOutput, calls=%fused_computation.7.clone.clone.1 | convolution fusion | flops 1684275200 | bytes 15074192 | tf_op jit(solution)/shard_map/while/body/eval_jaxpr/mab,mkbc->kac/dot_general | solution.py:95
  404.8 3.7 fusion.60
  412.1 18.5 %gather_fusion.1 = bf16[400,128,128]{2,1,0:T(8,128)(2,1)} fusion(bf16[540,128,128]{2,1,0:T(8,128)(2,1)} %get-tuple-element.328, s32[1024]{0:T(1024)S(1)} %pad_clamp_fusion.7), kind=kCustom, calls=%fused_computation.1.clone.clone.1 | custom fusion | bytes 26216000 | tf_op jit(solution)/shard_map/while/body/eval_jaxpr/jit(_take)/gather | solution.py:93
  430.6 17.7 %copy.62 = bf16[20,20,128,128]{2,3,0,1:T(8,128)(2,1)} copy(bf16[20,20,128,128]{3,2,1,0:T(8,128)(2,1)} %bitcast.84) | data formatting | bytes 26214400 | tf_op jit(solution)/shard_map/while/body/eval_jaxpr/jit(_take)/gather | solution.py:93
  448.4 8.4 %fusion.59 = f32[20,128,128]{2,1,0:T(8,128)S(1)} fusion(bf16[20,20,128,128]{2,3,0,1:T(8,128)(2,1)} %copy.62, pred[20,20]{0,1:T(8,128)(4,1)S(1)} %copy.63, bf16[3,20,128,128]{3,2,1,0:T(8,128)(2,1)} %get-tuple-element.329, s32[]{:T(128)} %get-tuple-element.312), kind=kOutput, calls=%fused_computation.7.clone.clone.1 | convolution fusion | flops 1684275200 | bytes 15074192 | tf_op jit(solution)/shard_map/while/body/eval_jaxpr/mab,mkbc->kac/dot_general | solution.py:95
  457.0 3.7 fusion.60
  (90 shorter events, 24.5 us)
Async XLA Ops:
  3.1 10.2 %copy-start.4 = (s32[768]{0:T(1024)S(1)}, s32[768]{0:T(1024)}, u32[]{:S(2)}) copy-start(s32[768]{0:T(1024)} %param.11) | copy-start | bytes 9220
  5.8 8.2 %copy-start.1 = (bf16[1,1,3,20,128,128]{5,4,3,2,1,0:T(8,128)(2,1)S(1)}, bf16[1,1,3,20,128,128]{5,4,3,2,1,0:T(8,128)(2,1)}, u32[]{:S(2)}) copy-start(bf16[1,1,3,20,128,128]{5,4,3,2,1,0:T(8,128)(2,1)} %param.7) | copy-start | bytes 5898244
  5.8 56.3 %all-to-all-start = ((bf16[32,2,16384]{2,1,0:T(2,128)(2,1)}), bf16[32,2,16384]{2,1,0:T(2,128)(2,1)}, u32[]{:S(2)}, u32[]{:S(2)}) async-start(bf16[32,2,16384]{2,1,0:T(2,128)(2,1)} %all_to_all.8), calls=%async_computation | async-start | bytes 4194304 | tf_op jit(solution)/shard_map/all_to_all | solution.py:69
  69.7 85.6 %collective-permute-start = (bf16[1,1,3,20,128,128]{5,4,3,2,1,0:T(8,128)(2,1)}, bf16[1,1,3,20,128,128]{5,4,3,2,1,0:T(8,128)(2,1)S(1)}, u32[]{:S(2)}, u32[]{:S(2)}) collective-permute-start(bf16[1,1,3,20,128,128]{5,4,3,2,1,0:T(8,128)(2,1)} %bitcast.29), channel_id=1, source_target_pairs={{0,4},{4,8},{8,12},{12,16},{16,20},{20,24},{24,28},{28,0},{1,5},{5... | collective-permute-start | bytes 5898248 | tf_op jit(solution)/shard_map/ppermute | solution.py:16
  71.0 88.8 %collective-permute-start.1 = (bf16[1,1,3,20,128,128]{5,4,3,2,1,0:T(8,128)(2,1)}, bf16[1,1,3,20,128,128]{5,4,3,2,1,0:T(8,128)(2,1)S(1)}, u32[]{:S(2)}, u32[]{:S(2)}) collective-permute-start(bf16[1,1,3,20,128,128]{5,4,3,2,1,0:T(8,128)(2,1)} %bitcast.29), channel_id=1, source_target_pairs={{4,0},{8,4},{12,8},{16,12},{20,16},{24,20},{28,24},{0,28},{5,1},{9... | collective-permute-start | bytes 5898248 | tf_op jit(solution)/shard_map/ppermute | solution.py:18
  156.8 6.2 %copy-start.3 = (s32[8,4,3,20]{3,1,2,0:T(4,128)S(1)}, s32[8,4,3,20]{3,1,2,0:T(4,128)}, u32[]{:S(2)}) copy-start(s32[8,4,3,20]{3,1,2,0:T(4,128)} %param.8) | copy-start | bytes 23044
  161.2 127.8 %collective-permute-start.2 = (bf16[3,1,3,20,128,128]{5,4,3,2,1,0:T(8,128)(2,1)}, bf16[3,1,3,20,128,128]{5,4,3,2,1,0:T(8,128)(2,1)}, u32[]{:S(2)}, u32[]{:S(2)}) collective-permute-start(bf16[3,1,3,20,128,128]{5,4,3,2,1,0:T(8,128)(2,1)} %constant_dynamic-update-slice_fusion.1), channel_id=1, source_target_pairs={{0,1},{1,2},{2,3},{3,0},{4,5},{5,6},{6,7},{7,4},{8,9},{9,10},{10,1... | collective-permute-start | bytes 17694728 | tf_op jit(solution)/shard_map/ppermute | solution.py:16
  161.2 128.7 %collective-permute-start.3 = (bf16[3,1,3,20,128,128]{5,4,3,2,1,0:T(8,128)(2,1)}, bf16[3,1,3,20,128,128]{5,4,3,2,1,0:T(8,128)(2,1)}, u32[]{:S(2)}, u32[]{:S(2)}) collective-permute-start(bf16[3,1,3,20,128,128]{5,4,3,2,1,0:T(8,128)(2,1)} %constant_dynamic-update-slice_fusion.1), channel_id=1, source_target_pairs={{1,0},{2,1},{3,2},{0,3},{5,4},{6,5},{7,6},{4,7},{9,8},{10,9},{11,1... | collective-permute-start | bytes 17694728 | tf_op jit(solution)/shard_map/ppermute | solution.py:18
  163.0 142.8 %copy-start.2 = (s32[8,4,3,20]{3,2,1,0:T(4,128)}, s32[8,4,3,20]{3,2,1,0:T(4,128)S(1)}, u32[]{:S(2)}) copy-start(s32[8,4,3,20]{3,2,1,0:T(4,128)S(1)} %copy.37) | copy-start | bytes 23044
  344.0 8.7 %copy-start = (bf16[20,20,128,128]{2,3,0,1:T(8,128)(2,1)S(1)}, bf16[20,20,128,128]{2,3,0,1:T(8,128)(2,1)}, u32[]{:S(2)}) copy-start(bf16[20,20,128,128]{2,3,0,1:T(8,128)(2,1)} %copy.62) | copy-start | bytes 39321604 | tf_op jit(solution)/shard_map/while
  396.2 8.7 %copy-start = (bf16[20,20,128,128]{2,3,0,1:T(8,128)(2,1)S(1)}, bf16[20,20,128,128]{2,3,0,1:T(8,128)(2,1)}, u32[]{:S(2)}) copy-start(bf16[20,20,128,128]{2,3,0,1:T(8,128)(2,1)} %copy.62) | copy-start | bytes 39321604 | tf_op jit(solution)/shard_map/while
  448.4 8.7 %copy-start = (bf16[20,20,128,128]{2,3,0,1:T(8,128)(2,1)S(1)}, bf16[20,20,128,128]{2,3,0,1:T(8,128)(2,1)}, u32[]{:S(2)}) copy-start(bf16[20,20,128,128]{2,3,0,1:T(8,128)(2,1)} %copy.62) | copy-start | bytes 39321604 | tf_op jit(solution)/shard_map/while
where the time goes:
time: 465 us; the launch traced here: 462 us
  waiting for transfers between devices  251 us (54%)
  local copies, waits for them, and re-layouts  136 us (29%)
  matrix products  41.1 us (9%)
  other arithmetic  19.9 us (4%)
  starting transfers between devices  13.9 us (3%)
    ppermute x2, waiting for transfers between devices, with_halo(): lax.ppermute(tail, axis, [(i, (i + 1) % count) for i in range(count)])  207 us
    gather x6, local copies, waits for them, and re-layouts, purify_row(): jnp.take(table, position.reshape(-1), axis=0, mode='fill', fill_value=0)  109 us
    all_to_all x1, waiting for transfers between devices, per_device(): lax.all_to_all(outgoing, ('gx', 'gy'), split_axis=0, concat_axis=0, tiled...  43.3 us
    dot_general x3, matrix products, purify_row(): jnp.einsum('mab,mkbc->kac', left_blocks, gathered, preferred_element_type...  25.1 us
    concatenate x1, other arithmetic, with_halo(): jnp.concatenate([lax.ppermute(tail, axis, [(i, (i + 1) % count) for i in...  15.8 us
    unnamed x15, local copies, waits for them, and re-layouts  11.3 us
    dot_general x3, matrix products, purify_row(): jnp.einsum('mab,mkbc->kac', square.astype(jnp.bfloat16), gathered, prefer...  11.2 us
  transfers between devices with their start and end apart: 5, of which 4 were waited for; matrix products, arithmetic and copies ran while one was open for 2% of the time, Pallas kernels for 0%

commit v1 on v0

v1 whole, which is shorter than its diff:
```python
import functools

import jax
import jax.numpy as jnp
from jax import lax
from jax.experimental import pallas as pl
from jax.experimental.pallas import tpu as pltpu
from jax.sharding import PartitionSpec as P

C = 2
MIB = 1024 * 1024


def pack_kernel(index_ref, ent_ref, out_ref):
    def body(i, carry):
        out_ref[i] = ent_ref[index_ref[i]]
        return carry

    lax.fori_loop(0, out_ref.shape[0], body, 0)


def admit_kernel(place_ref, inverse_ref, received_ref, density_ref, own_ref, total):
    rows, slots = inverse_ref.shape[0], density_ref.shape[0] // inverse_ref.shape[0]
    width = density_ref.shape[1]

    def widen(i, carry):
        total[i] = density_ref[i].astype(jnp.float32)
        return carry

    lax.fori_loop(0, density_ref.shape[0], widen, 0)

    def add(j, carry):
        place = place_ref[j]

        @pl.when(place >= 0)
        def _():
            total[place] += received_ref[j].astype(jnp.float32)

        return carry

    lax.fori_loop(0, received_ref.shape[0], add, 0)

    def spread(near, carry):
        for r in range(rows):
            for c in range(rows):
                slot = inverse_ref[r, near * rows + c]
                spot = (near, pl.ds(r * width, width), pl.ds(c * width, width))

                @pl.when(slot >= 0)
                def _():
                    own_ref[spot] = total[r * slots + slot].astype(jnp.bfloat16)

                @pl.when(slot < 0)
                def _():
                    own_ref[spot] = jnp.zeros((width, width), jnp.bfloat16)

        return carry

    lax.fori_loop(0, 9, spread, 0)


def purify_kernel(pieces_of, rows, slots, inverse_ref, *refs):
    count = 1 + max(p for p, _ in pieces_of.values())
    pieces = refs[:count]
    out_ref, left, right, square, square_b, sem = refs[count:]
    side = left.shape[0]
    width = side // rows
    copies = []
    for near in range(9):
        copies.append(
            pltpu.make_async_copy(
                pieces[0].at[near], left.at[:, pl.ds(near * side, side)], sem.at[len(copies)]
            )
        )
    for (m, c), (p, spot) in pieces_of.items():
        copies.append(
            pltpu.make_async_copy(
                pieces[p].at[spot], right.at[c, pl.ds(m * side, side), :], sem.at[len(copies)]
            )
        )
    for copy in copies:
        copy.start()
    for copy in copies:
        copy.wait()

    def product(lhs, c):
        cx, cy = c // 3, c % 3
        low_x, high_x = max(cx - 1, 0), min(cx + 1, 2)
        if cy == 1:
            spans = [(low_x * 3, (high_x + 1) * 3)]
        else:
            low_y, high_y = max(cy - 1, 0), min(cy + 1, 2)
            spans = [(mx * 3 + low_y, mx * 3 + high_y + 1) for mx in range(low_x, high_x + 1)]
        total = None
        for start, stop in spans:
            span = pl.ds(start * side, (stop - start) * side)
            term = jnp.dot(
                lhs[:, span], right[c, span, :], preferred_element_type=jnp.float32
            )
            total = term if total is None else total + term
        return total

    for c in range(9):
        square[c] = product(left, c)
        for r in range(rows):
            for q in range(rows):
                listed = inverse_ref[r, c * rows + q] >= 0
                down, across = pl.ds(r * width, width), pl.ds(q * width, width)
                tile = square[c, down, across]
                square_b[down, pl.ds(c * side + q * width, width)] = jnp.where(
                    listed, tile, jnp.zeros_like(tile)
                ).astype(jnp.bfloat16)
    for c in range(9):
        square[c] = 3.0 * square[c] - 2.0 * product(square_b, c)
        for r in range(rows):
            for q in range(rows):
                slot = inverse_ref[r, c * rows + q]

                @pl.when(slot >= 0)
                def _():
                    out_ref[r * slots + slot] = square[
                        c, pl.ds(r * width, width), pl.ds(q * width, width)
                    ]


def in_vmem():
    return pl.BlockSpec(memory_space=pltpu.VMEM)


def in_smem():
    return pl.BlockSpec(memory_space=pltpu.SMEM)


def shift(cells, axis, step):
    count = lax.axis_size(axis)
    return lax.ppermute(cells, axis, [(i, (i + step) % count) for i in range(count)])


def per_device(density, neighbours, ent_blocks, ent_owner, ent_place):
    wide_count = lax.axis_size("gx")
    narrow_count = lax.axis_size("gy")
    device_count = wide_count * narrow_count
    here_x = lax.axis_index("gx")
    here_y = lax.axis_index("gy")
    self_index = here_x * narrow_count + here_y
    rows, slots, width = density.shape[2:5]
    side = rows * width
    held = ent_blocks.shape[0]

    owners = ent_owner.reshape(device_count, held)
    places = ent_place.reshape(device_count, held)
    entry_ids = jnp.arange(held, dtype=jnp.int32)
    my_owners = lax.dynamic_index_in_dim(owners, self_index, 0, False)
    earlier = entry_ids[None, :] < entry_ids[:, None]
    my_ranks = jnp.sum((my_owners[:, None] == my_owners[None, :]) & earlier, axis=1)
    send_slot = my_owners * C + my_ranks
    buffer_ids = jnp.arange(device_count * C, dtype=jnp.int32)
    send_index = jnp.sum(
        jnp.where(buffer_ids[:, None] == send_slot[None, :], entry_ids[None, :], 0), axis=1
    ).astype(jnp.int32)
    for_me = owners == self_index
    my_rank_at = jnp.sum(for_me[:, None, :] & earlier[None, :, :], axis=2)
    capacity_ids = jnp.arange(C, dtype=jnp.int32)
    picked = for_me[:, :, None] & (my_rank_at[:, :, None] == capacity_ids[None, None, :])
    slot_place = (
        jnp.sum(jnp.where(picked, places[:, :, None] + 1, 0), axis=1).reshape(-1) - 1
    ).astype(jnp.int32)

    columns = lax.dynamic_index_in_dim(
        lax.dynamic_index_in_dim(neighbours, here_x, 0, False), here_y, 0, False
    )
    near_x = (columns // (narrow_count * rows) - here_x + 1) % wide_count
    near_y = (columns // rows % narrow_count - here_y + 1) % narrow_count
    spot = (near_x * 3 + near_y) * rows + columns % rows
    slot_ids = jnp.arange(slots, dtype=jnp.int32)
    spot_ids = jnp.arange(9 * rows, dtype=jnp.int32)
    inverse = (
        jnp.sum(
            jnp.where(spot[:, :, None] == spot_ids[None, None, :], slot_ids[None, :, None] + 1, 0),
            axis=1,
        )
        - 1
    ).astype(jnp.int32)

    outgoing = pl.pallas_call(
        pack_kernel,
        out_shape=jax.ShapeDtypeStruct((device_count * C, width, width), jnp.bfloat16),
        in_specs=[in_smem(), in_vmem()],
        out_specs=in_vmem(),
        compiler_params=pltpu.CompilerParams(vmem_limit_bytes=32 * MIB),
        name="pack",
    )(send_index, ent_blocks)
    received = lax.all_to_all(outgoing, ("gx", "gy"), split_axis=0, concat_axis=0, tiled=True)
    own = pl.pallas_call(
        admit_kernel,
        out_shape=jax.ShapeDtypeStruct((9, side, side), jnp.bfloat16),
        in_specs=[in_smem(), in_smem(), in_vmem(), in_vmem()],
        out_specs=in_vmem(),
        scratch_shapes=[pltpu.VMEM((rows * slots, width, width), jnp.float32)],
        compiler_params=pltpu.CompilerParams(vmem_limit_bytes=40 * MIB),
        name="admit",
    )(slot_place, inverse, received, density.reshape(rows * slots, width, width))

    own_grid = own.reshape(3, 3, side, side)
    pieces, pieces_of = [own], {(4, c): (0, (c,)) for c in range(9)}

    def keep(piece, mx, my, column_xs, column_ys):
        pieces.append(piece)
        for i, cx in enumerate(column_xs):
            for j, cy in enumerate(column_ys):
                pieces_of[(mx * 3 + my, cx * 3 + cy)] = (len(pieces) - 1, (i, j))

    for step in (1, -1):
        low = 1 if step == 1 else 0
        sent = lax.slice_in_dim(own_grid, low, low + 2, axis=1)
        keep(shift(sent, "gy", step), 1, 1 - step, (0, 1, 2), (1 - low, 2 - low))
    for part in (0, 1):
        for step_x in (1, -1):
            low_x = 1 if step_x == 1 else 0
            sent = lax.slice_in_dim(own_grid, low_x + part, low_x + part + 1, axis=0)
            edge = shift(sent, "gx", step_x)
            cx = low_x + part + (-1 if step_x == 1 else 1)
            mx = 1 - step_x
            keep(edge, mx, 1, (cx,), (0, 1, 2))
            for step in (1, -1):
                low = 1 if step == 1 else 0
                corner = lax.slice_in_dim(edge, low, low + 2, axis=1)
                keep(shift(corner, "gy", step), mx, 1 - step, (cx,), (1 - low, 2 - low))
    return run_purify(pieces, pieces_of, inverse, rows, slots, width, density.shape)


def run_purify(pieces, pieces_of, inverse, rows, slots, width, shape):
    side = rows * width
    purified = pl.pallas_call(
        functools.partial(purify_kernel, pieces_of, rows, slots),
        out_shape=jax.ShapeDtypeStruct((rows * slots, width, width), jnp.float32),
        in_specs=[in_smem()] + [pl.BlockSpec(memory_space=pl.ANY)] * len(pieces),
        out_specs=in_vmem(),
        scratch_shapes=[
            pltpu.VMEM((side, 9 * side), jnp.bfloat16),
            pltpu.VMEM((9, 9 * side, side), jnp.bfloat16),
            pltpu.VMEM((9, side, side), jnp.float32),
            pltpu.VMEM((side, 9 * side), jnp.bfloat16),
            pltpu.SemaphoreType.DMA((9 + len(pieces_of),)),
        ],
        compiler_params=pltpu.CompilerParams(vmem_limit_bytes=56 * MIB),
        name="purify",
    )(inverse, *pieces)
    return purified.reshape(shape)


def solution(mesh):
    in_specs = (P("gx", "gy", None, None, None, None), P(), P(("gx", "gy"), None, None), P(), P())
    out_specs = P("gx", "gy", None, None, None, None)
    return jax.shard_map(
        per_device, mesh=mesh, in_specs=in_specs, out_specs=out_specs, check_vma=False
    )
```

time: 465 us -> 247 us (0.53)
  local copies, waits for them, and re-layouts: 136 us -> 10.6 us
  waiting for transfers between devices: 251 us -> 183 us
  matrix products: 41.1 us -> 0 us
  Pallas kernels: 0 us -> 30.8 us
  other arithmetic: 19.9 us -> 1.35 us
  starting transfers between devices: 13.9 us -> 21 us
    gather x9 -> x0, local copies, waits for them, and re-layouts: 110 us -> none  [the longest x6 109 us: purify_row(): jnp.take(table, position.reshape(-1), axis=0, mode='fill', fill_value=0)]
    ppermute x4 -> x14, waiting for transfers between devices: 208 us -> 135 us  [shift(): lax.ppermute(cells, axis, [(i, (i + step) % count) for i in range(count)])]
    dot_general x8 -> x0, matrix products: 41.1 us -> none  [the longest x3 25.1 us: purify_row(): jnp.einsum('mab,mkbc->kac', left_blocks, gathered, preferred_element_type...]
    pallas_call x0 -> x3, Pallas kernels: none -> 30.8 us  [the longest x1 26.4 us: run_purify(): pl.pallas_call(functools.partial(purify_kernel, pieces_of, rows, slots),...]
    concatenate x1 -> x0, other arithmetic: 15.8 us -> none  [with_halo(): jnp.concatenate([lax.ppermute(tail, axis, [(i, (i + 1) % count) for i in...]
    ppermute x4 -> x14, starting transfers between devices: 6.47 us -> 13.7 us  [shift(): lax.ppermute(cells, axis, [(i, (i + step) % count) for i in range(count)])]
    all_to_all x2 -> x0, local copies, waits for them, and re-layouts: 5.37 us -> none  [per_device(): lax.all_to_all(outgoing, ('gx', 'gy'), split_axis=0, concat_axis=0, tiled...]
    dynamic_update_slice x6 -> x0, local copies, waits for them, and re-layouts: 4.66 us -> none  [per_device(): purified = lax.map(purify_row, (admitted[0, 0], my_columns))]
  transfers between devices with their start and end apart: 5 -> 15, of which waited for: 4 -> 9; matrix products, arithmetic and copies ran while one was open for 2% -> 1% of each run, Pallas kernels for 0% -> 0%
where the time goes in v1:
time: 247 us
  waiting for transfers between devices  183 us (74%)
  Pallas kernels  30.8 us (12%)
  starting transfers between devices  21 us (9%)
  local copies, waits for them, and re-layouts  10.6 us (4%)
    ppermute x14, waiting for transfers between devices, shift(): lax.ppermute(cells, axis, [(i, (i + step) % count) for i in range(count)])  135 us
    all_to_all x1, waiting for transfers between devices, per_device(): lax.all_to_all(outgoing, ('gx', 'gy'), split_axis=0, concat_axis=0, tiled...  47.3 us
    pallas_call x1, Pallas kernels, run_purify(): pl.pallas_call(functools.partial(purify_kernel, pieces_of, rows, slots),...  26.4 us
    ppermute x14, starting transfers between devices, shift(): lax.ppermute(cells, axis, [(i, (i + step) % count) for i in range(count)])  13.7 us
    unnamed x40, local copies, waits for them, and re-layouts  8.24 us
    all_to_all x1, starting transfers between devices, per_device(): lax.all_to_all(outgoing, ('gx', 'gy'), split_axis=0, concat_axis=0, tiled...  7.3 us
  transfers between devices with their start and end apart: 15, of which 9 were waited for; matrix products, arithmetic and copies ran while one was open for 1% of the time, Pallas kernels for 0%

profile of v1, /device:TPU:0, one launch (start us, length us, event | category | flops | bytes accessed | tf_op | source)
XLA Modules:
  0.0 246.9 jit_solution(13359003379982777987)
XLA Ops:
  1.1 1.1 copy-done.3
  2.2 1.0 pack.1
  3.2 1.3 copy-done.1
  4.5 7.3 %all-to-all-start = ((bf16[64,128,128]{2,1,0:T(8,128)(2,1)}), bf16[64,128,128]{2,1,0:T(8,128)(2,1)S(1)}, u32[]{:S(2)}, u32[]{:S(2)}) async-start(bf16[64,128,128]{2,1,0:T(8,128)(2,1)} %copy-done.1), calls=%async_computation | async-start | bytes 4194304 | tf_op jit(solution)/shard_map/all_to_all | solution.py:193
  13.4 47.3 %all-to-all-done.received_ref = bf16[64,128,128]{2,1,0:T(8,128)(2,1)S(1)} async-done(((bf16[64,128,128]{2,1,0:T(8,128)(2,1)}), bf16[64,128,128]{2,1,0:T(8,128)(2,1)S(1)}, u32[]{:S(2)}, u32[]{:S(2)}) %all-to-all-start) | async-done | bytes 2097184 | tf_op jit(solution)/shard_map/all_to_all | solution.py:193
  60.7 1.5 copy-done.2
  62.3 3.5 %admit.1.refs_0_ = bf16[9,384,384]{2,1,0:T(8,128)(2,1)S(1)} custom-call(s32[64]{0:T(128)S(1)} %sub.48.place_ref, s32[3,27]{1,0:T(4,128)S(1)} %broadcast_add_fusion.1.inverse_ref, bf16[64,128,128]{2,1,0:T(8,128)(2,1)S(1)} %all-to-all-done.received_ref, bf16[60,128,128]{2,1,0:T(8,128)(2,1)S(1)} %bitcast.51), custom_call_target="tpu_custom_call" | custom-call | tf_op jit(solution)/shard_map/admit/pallas_call | solution.py:194
  66.1 1.3 collective-permute-start.2
  67.4 3.4 %collective-permute-start.5 = (bf16[1,3,384,384]{3,2,1,0:T(8,128)(2,1)S(1)}, bf16[1,3,384,384]{3,2,1,0:T(8,128)(2,1)S(1)}, u32[]{:S(2)}, u32[]{:S(2)}) collective-permute-start(bf16[1,3,384,384]{3,2,1,0:T(8,128)(2,1)S(1)} %get-tuple-element.8), channel_id=1, source_target_pairs={{0,28},{4,0},{8,4},{12,8},{16,12},{20,16},{24,20},{28,24},{1,29},{... | collective-permute-start | bytes 2654216 | tf_op jit(solution)/shard_map/ppermute | solution.py:136
  70.9 2.0 collective-permute-start.8
  72.9 52.5 %collective-permute-done.2.refs_3_ = bf16[1,3,384,384]{3,2,1,0:T(8,128)(2,1)S(1)} collective-permute-done((bf16[1,3,384,384]{3,2,1,0:T(8,128)(2,1)S(1)}, bf16[1,3,384,384]{3,2,1,0:T(8,128)(2,1)S(1)}, u32[]{:S(2)}, u32[]{:S(2)}) %collective-permute-start.2) | collective-permute-done | bytes 884768 | tf_op jit(solution)/shard_map/ppermute | solution.py:136
  126.6 1.3 collective-permute-done.5.refs_6_
  128.1 17.1 %collective-permute-done.11.refs_12_ = bf16[1,3,384,384]{3,2,1,0:T(8,128)(2,1)S(1)} collective-permute-done((bf16[1,3,384,384]{3,2,1,0:T(8,128)(2,1)S(1)}, bf16[1,3,384,384]{3,2,1,0:T(8,128)(2,1)S(1)}, u32[]{:S(2)}, u32[]{:S(2)}) %collective-permute-start.11) | collective-permute-done | bytes 884768 | tf_op jit(solution)/shard_map/ppermute | solution.py:136
  146.1 1.1 collective-permute-start.13
  147.2 1.7 collective-permute-start.7
  149.1 32.8 %collective-permute-done.13.refs_14_ = bf16[1,2,384,384]{3,2,1,0:T(8,128)(2,1)S(1)} collective-permute-done((bf16[1,2,384,384]{3,2,1,0:T(8,128)(2,1)S(1)}, bf16[1,2,384,384]{3,2,1,0:T(8,128)(2,1)S(1)}, u32[]{:S(2)}, u32[]{:S(2)}) %collective-permute-start.13) | collective-permute-done | bytes 589856 | tf_op jit(solution)/shard_map/ppermute | solution.py:136
  181.9 3.1 %collective-permute-start.6 = (bf16[1,2,384,384]{3,2,1,0:T(8,128)(2,1)S(1)}, bf16[1,2,384,384]{3,2,1,0:T(8,128)(2,1)S(1)}, u32[]{:S(2)}, u32[]{:S(2)}) collective-permute-start(bf16[1,2,384,384]{3,2,1,0:T(8,128)(2,1)S(1)} %get-tuple-element.17), channel_id=1, source_target_pairs={{0,1},{1,2},{2,3},{3,0},{4,5},{5,6},{6,7},{7,4},{8,9},{9,10},{10,1... | collective-permute-start | bytes 1769480 | tf_op jit(solution)/shard_map/ppermute | solution.py:136
  184.9 13.2 %collective-permute-done.12.refs_13_ = bf16[1,2,384,384]{3,2,1,0:T(8,128)(2,1)S(1)} collective-permute-done((bf16[1,2,384,384]{3,2,1,0:T(8,128)(2,1)S(1)}, bf16[1,2,384,384]{3,2,1,0:T(8,128)(2,1)S(1)}, u32[]{:S(2)}, u32[]{:S(2)}) %collective-permute-start.12) | collective-permute-done | bytes 589856 | tf_op jit(solution)/shard_map/ppermute | solution.py:136
  198.6 10.0 %collective-permute-done.6.refs_7_ = bf16[1,2,384,384]{3,2,1,0:T(8,128)(2,1)S(1)} collective-permute-done((bf16[1,2,384,384]{3,2,1,0:T(8,128)(2,1)S(1)}, bf16[1,2,384,384]{3,2,1,0:T(8,128)(2,1)S(1)}, u32[]{:S(2)}, u32[]{:S(2)}) %collective-permute-start.6) | collective-permute-done | bytes 589856 | tf_op jit(solution)/shard_map/ppermute | solution.py:136
  208.6 3.3 %collective-permute-done.10.refs_11_ = bf16[1,2,384,384]{3,2,1,0:T(8,128)(2,1)S(1)} collective-permute-done((bf16[1,2,384,384]{3,2,1,0:T(8,128)(2,1)S(1)}, bf16[1,2,384,384]{3,2,1,0:T(8,128)(2,1)S(1)}, u32[]{:S(2)}, u32[]{:S(2)}) %collective-permute-start.10) | collective-permute-done | bytes 589856 | tf_op jit(solution)/shard_map/ppermute | solution.py:136
  211.9 5.2 %collective-permute-done.9.refs_10_ = bf16[1,2,384,384]{3,2,1,0:T(8,128)(2,1)S(1)} collective-permute-done((bf16[1,2,384,384]{3,2,1,0:T(8,128)(2,1)S(1)}, bf16[1,2,384,384]{3,2,1,0:T(8,128)(2,1)S(1)}, u32[]{:S(2)}, u32[]{:S(2)}) %collective-permute-start.9) | collective-permute-done | bytes 589856 | tf_op jit(solution)/shard_map/ppermute | solution.py:136
  218.0 1.2 copy-done.9
  219.2 1.2 copy-done.10
  220.4 26.4 %purify.1 = f32[60,128,128]{2,1,0:T(8,128)} custom-call(s32[3,27]{1,0:T(4,128)} %copy-done.4, bf16[9,384,384]{2,1,0:T(8,128)(2,1)} %copy-done, bf16[3,2,384,384]{3,2,1,0:T(8,128)(2,1)} %copy-done.10, bf16[3,2,384,384]{3,2,1,0:T(8,128)(2,1)} %copy-done.9, bf16[1,3,384,384]{3,2,1,0:T(8,128)(2,1)} %copy-done.5, bf16[1,2,384,384]{3,2,1,0:T(8,128)(2,1)} %copy-done.12, ...), custom_call_target="tpu_custom_call" | custom-call | tf_op jit(solution)/shard_map/purify/pallas_call | solution.py:234
  (78 shorter events, 6.6 us)
Async XLA Ops:
  4.5 56.2 %all-to-all-start = ((bf16[64,128,128]{2,1,0:T(8,128)(2,1)}), bf16[64,128,128]{2,1,0:T(8,128)(2,1)S(1)}, u32[]{:S(2)}, u32[]{:S(2)}) async-start(bf16[64,128,128]{2,1,0:T(8,128)(2,1)} %copy-done.1), calls=%async_computation | async-start | bytes 4194304 | tf_op jit(solution)/shard_map/all_to_all | solution.py:193
  13.4 52.4 %copy-start.4 = (s32[3,27]{1,0:T(4,128)}, s32[3,27]{1,0:T(4,128)S(1)}, u32[]{:S(2)}) copy-start(s32[3,27]{1,0:T(4,128)S(1)} %broadcast_add_fusion.1.inverse_ref) | copy-start | bytes 976
  65.8 59.8 %copy-start = (bf16[9,384,384]{2,1,0:T(8,128)(2,1)}, bf16[9,384,384]{2,1,0:T(8,128)(2,1)S(1)}, u32[]{:S(2)}) copy-start(bf16[9,384,384]{2,1,0:T(8,128)(2,1)S(1)} %admit.1.refs_0_) | copy-start | bytes 7962628
  66.1 59.3 %collective-permute-start.2 = (bf16[1,3,384,384]{3,2,1,0:T(8,128)(2,1)S(1)}, bf16[1,3,384,384]{3,2,1,0:T(8,128)(2,1)S(1)}, u32[]{:S(2)}, u32[]{:S(2)}) collective-permute-start(bf16[1,3,384,384]{3,2,1,0:T(8,128)(2,1)S(1)} %get-tuple-element.9), channel_id=1, source_target_pairs={{0,4},{4,8},{8,12},{12,16},{16,20},{20,24},{24,28},{28,0},{1,5},{5... | collective-permute-start | bytes 2654216 | tf_op jit(solution)/shard_map/ppermute | solution.py:136
  67.4 60.5 %collective-permute-start.5 = (bf16[1,3,384,384]{3,2,1,0:T(8,128)(2,1)S(1)}, bf16[1,3,384,384]{3,2,1,0:T(8,128)(2,1)S(1)}, u32[]{:S(2)}, u32[]{:S(2)}) collective-permute-start(bf16[1,3,384,384]{3,2,1,0:T(8,128)(2,1)S(1)} %get-tuple-element.8), channel_id=1, source_target_pairs={{0,28},{4,0},{8,4},{12,8},{16,12},{20,16},{24,20},{28,24},{1,29},{... | collective-permute-start | bytes 2654216 | tf_op jit(solution)/shard_map/ppermute | solution.py:136
  70.8 74.3 %collective-permute-start.11 = (bf16[1,3,384,384]{3,2,1,0:T(8,128)(2,1)S(1)}, bf16[1,3,384,384]{3,2,1,0:T(8,128)(2,1)S(1)}, u32[]{:S(2)}, u32[]{:S(2)}) collective-permute-start(bf16[1,3,384,384]{3,2,1,0:T(8,128)(2,1)S(1)} %get-tuple-element.9), channel_id=1, source_target_pairs={{0,28},{4,0},{8,4},{12,8},{16,12},{20,16},{24,20},{28,24},{1,29},{... | collective-permute-start | bytes 2654216 | tf_op jit(solution)/shard_map/ppermute | solution.py:136
  70.9 75.2 %collective-permute-start.8 = (bf16[1,3,384,384]{3,2,1,0:T(8,128)(2,1)S(1)}, bf16[1,3,384,384]{3,2,1,0:T(8,128)(2,1)S(1)}, u32[]{:S(2)}, u32[]{:S(2)}) collective-permute-start(bf16[1,3,384,384]{3,2,1,0:T(8,128)(2,1)S(1)} %get-tuple-element.7), channel_id=1, source_target_pairs={{0,4},{4,8},{8,12},{12,16},{16,20},{20,24},{24,28},{28,0},{1,5},{5... | collective-permute-start | bytes 2654216 | tf_op jit(solution)/shard_map/ppermute | solution.py:136
  125.5 21.7 %collective-permute-start.4 = (bf16[1,2,384,384]{3,2,1,0:T(8,128)(2,1)S(1)}, bf16[1,2,384,384]{3,2,1,0:T(8,128)(2,1)S(1)}, u32[]{:S(2)}, u32[]{:S(2)}) collective-permute-start(bf16[1,2,384,384]{3,2,1,0:T(8,128)(2,1)S(1)} %get-tuple-element.18), channel_id=1, source_target_pairs={{0,3},{1,0},{2,1},{3,2},{4,7},{5,4},{6,5},{7,6},{8,11},{9,8},{10,9... | collective-permute-start | bytes 1769480 | tf_op jit(solution)/shard_map/ppermute | solution.py:136
  126.3 20.9 %collective-permute-start.3 = (bf16[1,2,384,384]{3,2,1,0:T(8,128)(2,1)S(1)}, bf16[1,2,384,384]{3,2,1,0:T(8,128)(2,1)S(1)}, u32[]{:S(2)}, u32[]{:S(2)}) collective-permute-start(bf16[1,2,384,384]{3,2,1,0:T(8,128)(2,1)S(1)} %get-tuple-element.19), channel_id=1, source_target_pairs={{0,1},{1,2},{2,3},{3,0},{4,5},{5,6},{6,7},{7,4},{8,9},{9,10},{10,1... | collective-permute-start | bytes 1769480 | tf_op jit(solution)/shard_map/ppermute | solution.py:136
  127.9 17.5 %copy-start.6 = (bf16[1,3,384,384]{3,2,1,0:T(8,128)(2,1)}, bf16[1,3,384,384]{3,2,1,0:T(8,128)(2,1)S(1)}, u32[]{:S(2)}) copy-start(bf16[1,3,384,384]{3,2,1,0:T(8,128)(2,1)S(1)} %collective-permute-done.5.refs_6_) | copy-start | bytes 2654212
  127.9 89.2 %collective-permute-start.1 = (bf16[3,2,384,384]{3,2,1,0:T(8,128)(2,1)S(1)}, bf16[3,2,384,384]{3,2,1,0:T(8,128)(2,1)S(1)}, u32[]{:S(2)}, u32[]{:S(2)}) collective-permute-start(bf16[3,2,384,384]{3,2,1,0:T(8,128)(2,1)S(1)} %get-tuple-element.10), channel_id=1, source_target_pairs={{0,3},{1,0},{2,1},{3,2},{4,7},{5,4},{6,5},{7,6},{8,11},{9,8},{10,9... | collective-permute-start | bytes 5308424 | tf_op jit(solution)/shard_map/ppermute | solution.py:136
  145.2 72.8 %collective-permute-start = (bf16[3,2,384,384]{3,2,1,0:T(8,128)(2,1)S(1)}, bf16[3,2,384,384]{3,2,1,0:T(8,128)(2,1)S(1)}, u32[]{:S(2)}, u32[]{:S(2)}) collective-permute-start(bf16[3,2,384,384]{3,2,1,0:T(8,128)(2,1)S(1)} %get-tuple-element.11), channel_id=1, source_target_pairs={{0,1},{1,2},{2,3},{3,0},{4,5},{5,6},{6,7},{7,4},{8,9},{9,10},{10,1... | collective-permute-start | bytes 5308424 | tf_op jit(solution)/shard_map/ppermute | solution.py:136
  146.1 71.8 %copy-start.8 = (bf16[1,3,384,384]{3,2,1,0:T(8,128)(2,1)}, bf16[1,3,384,384]{3,2,1,0:T(8,128)(2,1)S(1)}, u32[]{:S(2)}) copy-start(bf16[1,3,384,384]{3,2,1,0:T(8,128)(2,1)S(1)} %collective-permute-done.8.refs_9_) | copy-start | bytes 2654212
  146.1 35.8 %collective-permute-start.13 = (bf16[1,2,384,384]{3,2,1,0:T(8,128)(2,1)S(1)}, bf16[1,2,384,384]{3,2,1,0:T(8,128)(2,1)S(1)}, u32[]{:S(2)}, u32[]{:S(2)}) collective-permute-start(bf16[1,2,384,384]{3,2,1,0:T(8,128)(2,1)S(1)} %get-tuple-element.12), channel_id=1, source_target_pairs={{0,3},{1,0},{2,1},{3,2},{4,7},{5,4},{6,5},{7,6},{8,11},{9,8},{10,9... | collective-permute-start | bytes 1769480 | tf_op jit(solution)/shard_map/ppermute | solution.py:136
  147.2 70.7 %copy-start.11 = (bf16[1,2,384,384]{3,2,1,0:T(8,128)(2,1)}, bf16[1,2,384,384]{3,2,1,0:T(8,128)(2,1)S(1)}, u32[]{:S(2)}) copy-start(bf16[1,2,384,384]{3,2,1,0:T(8,128)(2,1)S(1)} %collective-permute-done.4.refs_5_) | copy-start | bytes 1769476
  147.2 50.9 %collective-permute-start.12 = (bf16[1,2,384,384]{3,2,1,0:T(8,128)(2,1)S(1)}, bf16[1,2,384,384]{3,2,1,0:T(8,128)(2,1)S(1)}, u32[]{:S(2)}, u32[]{:S(2)}) collective-permute-start(bf16[1,2,384,384]{3,2,1,0:T(8,128)(2,1)S(1)} %get-tuple-element.13), channel_id=1, source_target_pairs={{0,1},{1,2},{2,3},{3,0},{4,5},{5,6},{6,7},{7,4},{8,9},{9,10},{10,1... | collective-permute-start | bytes 1769480 | tf_op jit(solution)/shard_map/ppermute | solution.py:136
  147.2 70.7 %copy-start.12 = (bf16[1,2,384,384]{3,2,1,0:T(8,128)(2,1)}, bf16[1,2,384,384]{3,2,1,0:T(8,128)(2,1)S(1)}, u32[]{:S(2)}) copy-start(bf16[1,2,384,384]{3,2,1,0:T(8,128)(2,1)S(1)} %collective-permute-done.3.refs_4_) | copy-start | bytes 1769476
  147.2 50.9 %collective-permute-start.7 = (bf16[1,2,384,384]{3,2,1,0:T(8,128)(2,1)S(1)}, bf16[1,2,384,384]{3,2,1,0:T(8,128)(2,1)S(1)}, u32[]{:S(2)}, u32[]{:S(2)}) collective-permute-start(bf16[1,2,384,384]{3,2,1,0:T(8,128)(2,1)S(1)} %get-tuple-element.16), channel_id=1, source_target_pairs={{0,3},{1,0},{2,1},{3,2},{4,7},{5,4},{6,5},{7,6},{8,11},{9,8},{10,9... | collective-permute-start | bytes 1769480 | tf_op jit(solution)/shard_map/ppermute | solution.py:136
  181.9 36.1 %copy-start.13 = (bf16[1,2,384,384]{3,2,1,0:T(8,128)(2,1)}, bf16[1,2,384,384]{3,2,1,0:T(8,128)(2,1)S(1)}, u32[]{:S(2)}) copy-start(bf16[1,2,384,384]{3,2,1,0:T(8,128)(2,1)S(1)} %collective-permute-done.13.refs_14_) | copy-start | bytes 1769476
  181.9 26.7 %collective-permute-start.6 = (bf16[1,2,384,384]{3,2,1,0:T(8,128)(2,1)S(1)}, bf16[1,2,384,384]{3,2,1,0:T(8,128)(2,1)S(1)}, u32[]{:S(2)}, u32[]{:S(2)}) collective-permute-start(bf16[1,2,384,384]{3,2,1,0:T(8,128)(2,1)S(1)} %get-tuple-element.17), channel_id=1, source_target_pairs={{0,1},{1,2},{2,3},{3,0},{4,5},{5,6},{6,7},{7,4},{8,9},{9,10},{10,1... | collective-permute-start | bytes 1769480 | tf_op jit(solution)/shard_map/ppermute | solution.py:136
  198.1 19.8 %copy-start.14 = (bf16[1,2,384,384]{3,2,1,0:T(8,128)(2,1)}, bf16[1,2,384,384]{3,2,1,0:T(8,128)(2,1)S(1)}, u32[]{:S(2)}) copy-start(bf16[1,2,384,384]{3,2,1,0:T(8,128)(2,1)S(1)} %collective-permute-done.12.refs_13_) | copy-start | bytes 1769476
  198.1 13.8 %collective-permute-start.10 = (bf16[1,2,384,384]{3,2,1,0:T(8,128)(2,1)S(1)}, bf16[1,2,384,384]{3,2,1,0:T(8,128)(2,1)S(1)}, u32[]{:S(2)}, u32[]{:S(2)}) collective-permute-start(bf16[1,2,384,384]{3,2,1,0:T(8,128)(2,1)S(1)} %get-tuple-element.14), channel_id=1, source_target_pairs={{0,3},{1,0},{2,1},{3,2},{4,7},{5,4},{6,5},{7,6},{8,11},{9,8},{10,9... | collective-permute-start | bytes 1769480 | tf_op jit(solution)/shard_map/ppermute | solution.py:136
  198.1 19.8 %copy-start.15 = (bf16[1,2,384,384]{3,2,1,0:T(8,128)(2,1)}, bf16[1,2,384,384]{3,2,1,0:T(8,128)(2,1)S(1)}, u32[]{:S(2)}) copy-start(bf16[1,2,384,384]{3,2,1,0:T(8,128)(2,1)S(1)} %collective-permute-done.7.refs_8_) | copy-start | bytes 1769476
  198.1 18.9 %collective-permute-start.9 = (bf16[1,2,384,384]{3,2,1,0:T(8,128)(2,1)S(1)}, bf16[1,2,384,384]{3,2,1,0:T(8,128)(2,1)S(1)}, u32[]{:S(2)}, u32[]{:S(2)}) collective-permute-start(bf16[1,2,384,384]{3,2,1,0:T(8,128)(2,1)S(1)} %get-tuple-element.15), channel_id=1, source_target_pairs={{0,1},{1,2},{2,3},{3,0},{4,5},{5,6},{6,7},{7,4},{8,9},{9,10},{10,1... | collective-permute-start | bytes 1769480 | tf_op jit(solution)/shard_map/ppermute | solution.py:136
  (11 other events, 31.1 us)

commit v2 on v1

--- a/solution.py
+++ b/solution.py
@@ -59,68 +59,137 @@
     lax.fori_loop(0, 9, spread, 0)
 
 
-def purify_kernel(pieces_of, rows, slots, inverse_ref, *refs):
-    count = 1 + max(p for p, _ in pieces_of.values())
-    pieces = refs[:count]
-    out_ref, left, right, square, square_b, sem = refs[count:]
+def exchange_kernel(
+    rows, gx_count, gy_count, own_ref, mask_ref, out_ref,
+    left, right, square, square_b, local_sem, send_sem, recv_sem,
+):
     side = left.shape[0]
     width = side // rows
-    copies = []
-    for near in range(9):
-        copies.append(
-            pltpu.make_async_copy(
-                pieces[0].at[near], left.at[:, pl.ds(near * side, side)], sem.at[len(copies)]
-            )
+    here_x, here_y = lax.axis_index("gx"), lax.axis_index("gy")
+    beside_x = {
+        1: (lax.rem(here_x + 1, gx_count), here_y),
+        -1: (lax.rem(here_x + gx_count - 1, gx_count), here_y),
+    }
+    beside_y = {
+        1: (here_x, lax.rem(here_y + 1, gy_count)),
+        -1: (here_x, lax.rem(here_y + gy_count - 1, gy_count)),
+    }
+
+    def tile(c, m):
+        return right.at[c, pl.ds(m * side, side), :]
+
+    local = [
+        pltpu.make_async_copy(own_ref.at[m], left.at[:, pl.ds(m * side, side)], local_sem.at[m])
+        for m in range(9)
+    ] + [
+        pltpu.make_async_copy(own_ref.at[c], tile(c, 4), local_sem.at[9 + c]) for c in range(9)
+    ]
+
+    sends = []
+
+    def send(source, c, m, device):
+        copy = pltpu.make_async_remote_copy(
+            src_ref=source,
+            dst_ref=tile(c, m),
+            send_sem=send_sem.at[len(sends)],
+            recv_sem=recv_sem.at[len(sends)],
+            device_id=device,
+            device_id_type=pl.DeviceIdType.MESH,
         )
-    for (m, c), (p, spot) in pieces_of.items():
-        copies.append(
-            pltpu.make_async_copy(
-                pieces[p].at[spot], right.at[c, pl.ds(m * side, side), :], sem.at[len(copies)]
-            )
-        )
-    for copy in copies:
+        sends.append(copy)
         copy.start()
-    for copy in copies:
+        return copy
+
+    barrier = pltpu.get_barrier_semaphore()
+    for device in (*beside_x.values(), *beside_y.values()):
+        pl.semaphore_signal(barrier, inc=1, device_id=device, device_id_type=pl.DeviceIdType.MESH)
+    pl.semaphore_wait(barrier, 4)
+
+    edges, sides = [], []
+    for qy in (1, 0, 2):
+        for part in (0, 1):
+            for step in (1, -1):
+                qx = part + 1 if step == 1 else part
+                cx, mx = qx - step, 1 - step
+                copy = send(own_ref.at[qx * 3 + qy], cx * 3 + qy, mx * 3 + 1, beside_x[step])
+                edges.append((copy, cx, qy, mx))
+                qy2 = part + 1 if step == 1 else part
+                line = (1, 0, 2).index(qy)
+                c2 = line * 3 + qy2 - step
+                sides.append(send(own_ref.at[line * 3 + qy2], c2, 3 + 1 - step, beside_y[step]))
+    for copy in local:
+        copy.start()
+
+    corners = []
+
+    def forward(edge):
+        copy, cx, cy, mx = edge
+        copy.wait_recv()
+        for step in (1, -1):
+            if 0 <= cy - step <= 2:
+                c = cx * 3 + cy
+                corners.append(
+                    send(tile(c, mx * 3 + 1), cx * 3 + cy - step, mx * 3 + 1 - step, beside_y[step])
+                )
+
+    def product(lhs, c, mx):
+        cy = c % 3
+        low_y, high_y = max(cy - 1, 0), min(cy + 1, 2)
+        span = pl.ds((mx * 3 + low_y) * side, (high_y - low_y + 1) * side)
+        return jnp.dot(lhs[:, span], right[c, span, :], preferred_element_type=jnp.float32)
+
+    for edge in edges[:8]:
+        forward(edge)
+    for copy in local:
         copy.wait()
-
-    def product(lhs, c):
-        cx, cy = c // 3, c % 3
-        low_x, high_x = max(cx - 1, 0), min(cx + 1, 2)
-        if cy == 1:
-            spans = [(low_x * 3, (high_x + 1) * 3)]
-        else:
-            low_y, high_y = max(cy - 1, 0), min(cy + 1, 2)
-            spans = [(mx * 3 + low_y, mx * 3 + high_y + 1) for mx in range(low_x, high_x + 1)]
-        total = None
-        for start, stop in spans:
-            span = pl.ds(start * side, (stop - start) * side)
-            term = jnp.dot(
-                lhs[:, span], right[c, span, :], preferred_element_type=jnp.float32
-            )
-            total = term if total is None else total + term
-        return total
-
+    for copy in sides:
+        copy.wait_recv()
     for c in range(9):
-        square[c] = product(left, c)
+        square[c] = product(left, c, 1)
+        if c % 2 == 0 and 8 + c // 2 < len(edges):
+            forward(edges[8 + c // 2])
+    for copy in corners:
+        copy.wait_recv()
+
+    for c in range(9):
+        total = square[c]
+        for mx in (0, 2):
+            if abs(mx - c // 3) <= 1:
+                total = total + product(left, c, mx)
+        square[c] = total
+        for r in range(rows):
+            down, across = pl.ds(r * width, width), pl.ds(c * side, side)
+            square_b[down, across] = (
+                square[c, down, :] * mask_ref[r : r + 1, across]
+            ).astype(jnp.bfloat16)
+    for c in range(9):
+        total = product(square_b, c, 1)
+        for mx in (0, 2):
+            if abs(mx - c // 3) <= 1:
+                total = total + product(square_b, c, mx)
+        total = 3.0 * square[c] - 2.0 * total
         for r in range(rows):
             for q in range(rows):
-                listed = inverse_ref[r, c * rows + q] >= 0
-                down, across = pl.ds(r * width, width), pl.ds(q * width, width)
-                tile = square[c, down, across]
-                square_b[down, pl.ds(c * side + q * width, width)] = jnp.where(
-                    listed, tile, jnp.zeros_like(tile)
-                ).astype(jnp.bfloat16)
-    for c in range(9):
-        square[c] = 3.0 * square[c] - 2.0 * product(square_b, c)
-        for r in range(rows):
-            for q in range(rows):
-                slot = inverse_ref[r, c * rows + q]
-
-                @pl.when(slot >= 0)
-                def _():
-                    out_ref[r * slots + slot] = square[
-                        c, pl.ds(r * width, width), pl.ds(q * width, width)
-                    ]
+                out_ref[(c * rows + q) * rows + r] = total[
+                    r * width : (r + 1) * width, q * width : (q + 1) * width
+                ]
+    for copy in sends:
+        copy.wait_send()
+
+
+def pick_kernel(index_ref, dense_ref, out_ref, sem):
+    count = out_ref.shape[0]
+
+    def start(i, carry):
+        pltpu.make_async_copy(dense_ref.at[index_ref[i]], out_ref.at[i], sem.at[i]).start()
+        return carry
+
+    def wait(i, carry):
+        pltpu.make_async_copy(dense_ref.at[index_ref[i]], out_ref.at[i], sem.at[i]).wait()
+        return carry
+
+    lax.fori_loop(0, count, start, 0)
+    lax.fori_loop(0, count, wait, 0)
 
 
 def in_vmem():
@@ -129,11 +198,6 @@
 
 def in_smem():
     return pl.BlockSpec(memory_space=pltpu.SMEM)
-
-
-def shift(cells, axis, step):
-    count = lax.axis_size(axis)
-    return lax.ppermute(cells, axis, [(i, (i + step) % count) for i in range(count)])
 
 
 def per_device(density, neighbours, ent_blocks, ent_owner, ent_place):
@@ -201,52 +265,37 @@
         name="admit",
     )(slot_place, inverse, received, density.reshape(rows * slots, width, width))
 
-    own_grid = own.reshape(3, 3, side, side)
-    pieces, pieces_of = [own], {(4, c): (0, (c,)) for c in range(9)}
-
-    def keep(piece, mx, my, column_xs, column_ys):
-        pieces.append(piece)
-        for i, cx in enumerate(column_xs):
-            for j, cy in enumerate(column_ys):
-                pieces_of[(mx * 3 + my, cx * 3 + cy)] = (len(pieces) - 1, (i, j))
-
-    for step in (1, -1):
-        low = 1 if step == 1 else 0
-        sent = lax.slice_in_dim(own_grid, low, low + 2, axis=1)
-        keep(shift(sent, "gy", step), 1, 1 - step, (0, 1, 2), (1 - low, 2 - low))
-    for part in (0, 1):
-        for step_x in (1, -1):
-            low_x = 1 if step_x == 1 else 0
-            sent = lax.slice_in_dim(own_grid, low_x + part, low_x + part + 1, axis=0)
-            edge = shift(sent, "gx", step_x)
-            cx = low_x + part + (-1 if step_x == 1 else 1)
-            mx = 1 - step_x
-            keep(edge, mx, 1, (cx,), (0, 1, 2))
-            for step in (1, -1):
-                low = 1 if step == 1 else 0
-                corner = lax.slice_in_dim(edge, low, low + 2, axis=1)
-                keep(shift(corner, "gy", step), mx, 1 - step, (cx,), (1 - low, 2 - low))
-    return run_purify(pieces, pieces_of, inverse, rows, slots, width, density.shape)
-
-
-def run_purify(pieces, pieces_of, inverse, rows, slots, width, shape):
-    side = rows * width
-    purified = pl.pallas_call(
-        functools.partial(purify_kernel, pieces_of, rows, slots),
-        out_shape=jax.ShapeDtypeStruct((rows * slots, width, width), jnp.float32),
-        in_specs=[in_smem()] + [pl.BlockSpec(memory_space=pl.ANY)] * len(pieces),
+    mask = jnp.repeat((inverse >= 0).astype(jnp.float32), width, axis=1)
+    dense = pl.pallas_call(
+        functools.partial(exchange_kernel, rows, wide_count, narrow_count),
+        out_shape=jax.ShapeDtypeStruct((9 * rows * rows, width, width), jnp.float32),
+        in_specs=[pl.BlockSpec(memory_space=pl.ANY), in_vmem()],
         out_specs=in_vmem(),
         scratch_shapes=[
             pltpu.VMEM((side, 9 * side), jnp.bfloat16),
             pltpu.VMEM((9, 9 * side, side), jnp.bfloat16),
             pltpu.VMEM((9, side, side), jnp.float32),
             pltpu.VMEM((side, 9 * side), jnp.bfloat16),
-            pltpu.SemaphoreType.DMA((9 + len(pieces_of),)),
+            pltpu.SemaphoreType.DMA((18,)),
+            pltpu.SemaphoreType.DMA((40,)),
+            pltpu.SemaphoreType.DMA((40,)),
         ],
-        compiler_params=pltpu.CompilerParams(vmem_limit_bytes=56 * MIB),
-        name="purify",
-    )(inverse, *pieces)
-    return purified.reshape(shape)
+        compiler_params=pltpu.CompilerParams(
+            vmem_limit_bytes=56 * MIB, collective_id=0, has_side_effects=True
+        ),
+        name="exchange",
+    )(own, mask)
+    row_ids = jnp.arange(rows, dtype=jnp.int32)
+    index = (spot * rows + row_ids[:, None]).reshape(-1).astype(jnp.int32)
+    purified = pl.pallas_call(
+        pick_kernel,
+        out_shape=jax.ShapeDtypeStruct((rows * slots, width, width), jnp.float32),
+        in_specs=[in_smem(), pl.BlockSpec(memory_space=pl.ANY)],
+        out_specs=pl.BlockSpec(memory_space=pl.ANY),
+        scratch_shapes=[pltpu.SemaphoreType.DMA((rows * slots,))],
+        name="pick",
+    )(index, dense)
+    return purified.reshape(density.shape)
 
 
 def solution(mesh):

time: 247 us -> 304 us (1.23); the launches traced: 247 us -> 298 us
  Pallas kernels: 30.8 us -> 236 us
  waiting for transfers between devices: 183 us -> 45.5 us
  starting transfers between devices: 21 us -> 7.3 us
    pallas_call x1 -> x2, Pallas kernels: 26.4 us -> 231 us  [the longest x1 121 us: per_device(): pl.pallas_call(pick_kernel, out_shape=jax.ShapeDtypeStruct((rows * slots,...]
    ppermute x14 -> x0, waiting for transfers between devices: 135 us -> none  [shift(): lax.ppermute(cells, axis, [(i, (i + step) % count) for i in range(count)])]
    ppermute x14 -> x0, starting transfers between devices: 13.7 us -> none  [shift(): lax.ppermute(cells, axis, [(i, (i + step) % count) for i in range(count)])]
    unnamed x40 -> x12, local copies, waits for them, and re-layouts: 8.24 us -> 6.21 us
  transfers between devices with their start and end apart: 15 -> 1, of which waited for: 9 -> 1; matrix products, arithmetic and copies ran while one was open for 1% -> 1% of each run, Pallas kernels for 0% -> 0%
where the time goes in v2:
time: 304 us; the launch traced here: 298 us
  Pallas kernels  236 us (78%)
  waiting for transfers between devices  45.5 us (15%)
  local copies, waits for them, and re-layouts  7.91 us (3%)
  starting transfers between devices  7.3 us (2%)
    pallas_call x1, Pallas kernels, per_device(): pl.pallas_call(pick_kernel, out_shape=jax.ShapeDtypeStruct((rows * slots,...  121 us
    pallas_call x1, Pallas kernels, per_device(): pl.pallas_call(functools.partial(exchange_kernel, rows, wide_count, narro...  110 us
    all_to_all x1, waiting for transfers between devices, per_device(): lax.all_to_all(outgoing, ('gx', 'gy'), split_axis=0, concat_axis=0, tiled...  45.5 us
    all_to_all x1, starting transfers between devices, per_device(): lax.all_to_all(outgoing, ('gx', 'gy'), split_axis=0, concat_axis=0, tiled...  7.3 us
    unnamed x12, local copies, waits for them, and re-layouts  6.21 us
  transfers between devices with their start and end apart: 1, of which 1 were waited for; matrix products, arithmetic and copies ran while one was open for 1% of the time, Pallas kernels for 0%

profile of v2, /device:TPU:0, one launch (start us, length us, event | category | flops | bytes accessed | tf_op | source)
XLA Modules:
  0.0 298.5 jit_solution(17082098350817493517)
XLA Ops:
  0.0 0.8 reshape.161
  0.8 0.2 convert_reduce_fusion.1
  1.0 0.1 select_reduce_fusion.2.index_ref
  1.1 1.1 copy-done.3
  2.2 1.0 pack.1
  3.2 1.3 copy-done.1
  4.5 7.3 %all-to-all-start = ((bf16[64,128,128]{2,1,0:T(8,128)(2,1)}), bf16[64,128,128]{2,1,0:T(8,128)(2,1)S(1)}, u32[]{:S(2)}, u32[]{:S(2)}) async-start(bf16[64,128,128]{2,1,0:T(8,128)(2,1)} %copy-done.1), calls=%async_computation | async-start | bytes 4194304 | tf_op jit(solution)/shard_map/all_to_all | solution.py:257
  11.9 0.1 add.168
  12.0 0.7 broadcast_remainder_fusion
  12.7 0.1 ne.130
  12.8 0.1 ne.127
  13.2 0.1 add.173
  13.4 0.2 convert_reduce_fusion
  13.6 0.1 copy.12
  13.7 0.1 sub.61.place_ref
  13.8 0.1 select_reduce_fusion
  14.0 0.6 copy.39
  14.6 0.5 multiply_add_fusion.index_ref
  15.2 45.5 %all-to-all-done.received_ref = bf16[64,128,128]{2,1,0:T(8,128)(2,1)S(1)} async-done(((bf16[64,128,128]{2,1,0:T(8,128)(2,1)}), bf16[64,128,128]{2,1,0:T(8,128)(2,1)S(1)}, u32[]{:S(2)}, u32[]{:S(2)}) %all-to-all-start) | async-done | bytes 2097184 | tf_op jit(solution)/shard_map/all_to_all | solution.py:257
  60.7 1.5 copy-done.2
  62.3 3.5 %admit.1.own_ref = bf16[9,384,384]{2,1,0:T(8,128)(2,1)S(1)} custom-call(s32[64]{0:T(128)S(1)} %sub.61.place_ref, s32[3,27]{1,0:T(4,128)S(1)} %broadcast_add_fusion.1.inverse_ref, bf16[64,128,128]{2,1,0:T(8,128)(2,1)S(1)} %all-to-all-done.received_ref, bf16[60,128,128]{2,1,0:T(8,128)(2,1)S(1)} %bitcast.48), custom_call_target="tpu_custom_call" | custom-call | tf_op jit(solution)/shard_map/admit/pallas_call | solution.py:258
  65.7 1.5 copy-done
  67.2 109.8 %exchange.1.dense_ref = f32[81,128,128]{2,1,0:T(8,128)} custom-call(bf16[9,384,384]{2,1,0:T(8,128)(2,1)} %copy-done, f32[3,3456]{1,0:T(4,128)} %bitcast.49), custom_call_target="tpu_custom_call" | custom-call | tf_op jit(solution)/shard_map/exchange/pallas_call | solution.py:269
  177.1 121.4 %pick.1 = f32[60,128,128]{2,1,0:T(8,128)} custom-call(s32[60]{0:T(128)} %multiply_add_fusion.index_ref, f32[81,128,128]{2,1,0:T(8,128)} %exchange.1.dense_ref), custom_call_target="tpu_custom_call" | custom-call | tf_op jit(solution)/shard_map/pick/pallas_call | solution.py:290
  (26 shorter events, 0.7 us)
Async XLA Ops:
  1.1 1.1 copy-start.3
  3.2 1.3 copy-start.1
  4.5 8.7 %copy-start.4 = (s32[768]{0:T(1024)S(1)}, s32[768]{0:T(1024)}, u32[]{:S(2)}) copy-start(s32[768]{0:T(1024)} %param.9) | copy-start | bytes 9220
  4.5 56.2 %all-to-all-start = ((bf16[64,128,128]{2,1,0:T(8,128)(2,1)}), bf16[64,128,128]{2,1,0:T(8,128)(2,1)S(1)}, u32[]{:S(2)}, u32[]{:S(2)}) async-start(bf16[64,128,128]{2,1,0:T(8,128)(2,1)} %copy-done.1), calls=%async_computation | async-start | bytes 4194304 | tf_op jit(solution)/shard_map/all_to_all | solution.py:257
  60.7 1.5 copy-start.2
  65.7 1.5 copy-start

commit v3 on v2

--- a/solution.py
+++ b/solution.py
@@ -105,18 +105,28 @@
         pl.semaphore_signal(barrier, inc=1, device_id=device, device_id_type=pl.DeviceIdType.MESH)
     pl.semaphore_wait(barrier, 4)
 
-    edges, sides = [], []
-    for qy in (1, 0, 2):
+    pairs = [(qy, part) for qy in (1, 0, 2) for part in (0, 1)]
+    edges = []
+
+    def send_pair(j):
+        qy, part = pairs[j]
+        pair = []
+        for step in (1, -1):
+            qx = part + 1 if step == 1 else part
+            cx, mx = qx - step, 1 - step
+            copy = send(own_ref.at[qx * 3 + qy], cx * 3 + qy, mx * 3 + 1, beside_x[step])
+            pair.append((copy, cx, qy, mx))
+        edges.append(pair)
+
+    send_pair(0)
+    send_pair(1)
+    sides = []
+    for qx in (1, 0, 2):
         for part in (0, 1):
             for step in (1, -1):
-                qx = part + 1 if step == 1 else part
-                cx, mx = qx - step, 1 - step
-                copy = send(own_ref.at[qx * 3 + qy], cx * 3 + qy, mx * 3 + 1, beside_x[step])
-                edges.append((copy, cx, qy, mx))
-                qy2 = part + 1 if step == 1 else part
-                line = (1, 0, 2).index(qy)
-                c2 = line * 3 + qy2 - step
-                sides.append(send(own_ref.at[line * 3 + qy2], c2, 3 + 1 - step, beside_y[step]))
+                qy = part + 1 if step == 1 else part
+                c = qx * 3 + qy - step
+                sides.append(send(own_ref.at[qx * 3 + qy], c, 4 - step, beside_y[step]))
     for copy in local:
         copy.start()
 
@@ -138,16 +148,24 @@
         span = pl.ds((mx * 3 + low_y) * side, (high_y - low_y + 1) * side)
         return jnp.dot(lhs[:, span], right[c, span, :], preferred_element_type=jnp.float32)
 
-    for edge in edges[:8]:
-        forward(edge)
+    def turn(j):
+        for edge in edges[j]:
+            edge[0].wait_send()
+        if j + 2 < len(pairs):
+            send_pair(j + 2)
+        for edge in edges[j]:
+            forward(edge)
+
+    for j in range(4):
+        turn(j)
     for copy in local:
         copy.wait()
     for copy in sides:
         copy.wait_recv()
     for c in range(9):
         square[c] = product(left, c, 1)
-        if c % 2 == 0 and 8 + c // 2 < len(edges):
-            forward(edges[8 + c // 2])
+        if c in (1, 5):
+            turn(4 + c // 4)
     for copy in corners:
         copy.wait_recv()
 
@@ -173,23 +191,16 @@
                 out_ref[(c * rows + q) * rows + r] = total[
                     r * width : (r + 1) * width, q * width : (q + 1) * width
                 ]
-    for copy in sends:
+    for copy in sides + corners:
         copy.wait_send()
 
 
-def pick_kernel(index_ref, dense_ref, out_ref, sem):
-    count = out_ref.shape[0]
-
-    def start(i, carry):
-        pltpu.make_async_copy(dense_ref.at[index_ref[i]], out_ref.at[i], sem.at[i]).start()
-        return carry
-
-    def wait(i, carry):
-        pltpu.make_async_copy(dense_ref.at[index_ref[i]], out_ref.at[i], sem.at[i]).wait()
-        return carry
-
-    lax.fori_loop(0, count, start, 0)
-    lax.fori_loop(0, count, wait, 0)
+def pick_kernel(index_ref, dense_ref, out_ref):
+    def body(i, carry):
+        out_ref[i] = dense_ref[index_ref[i]]
+        return carry
+
+    lax.fori_loop(0, out_ref.shape[0], body, 0)
 
 
 def in_vmem():
@@ -290,9 +301,9 @@
     purified = pl.pallas_call(
         pick_kernel,
         out_shape=jax.ShapeDtypeStruct((rows * slots, width, width), jnp.float32),
-        in_specs=[in_smem(), pl.BlockSpec(memory_space=pl.ANY)],
-        out_specs=pl.BlockSpec(memory_space=pl.ANY),
-        scratch_shapes=[pltpu.SemaphoreType.DMA((rows * slots,))],
+        in_specs=[in_smem(), in_vmem()],
+        out_specs=in_vmem(),
+        compiler_params=pltpu.CompilerParams(vmem_limit_bytes=32 * MIB),
         name="pick",
     )(index, dense)
     return purified.reshape(density.shape)

time: 304 us -> 183 us (0.60); the launches traced: 298 us -> 183 us
  Pallas kernels: 236 us -> 117 us
    pallas_call x1, Pallas kernels: 121 us -> 3 us  [per_device(): pl.pallas_call(pick_kernel, out_shape=jax.ShapeDtypeStruct((rows * slots,...]
    unnamed x12 -> x14, local copies, waits for them, and re-layouts: 6.21 us -> 8.7 us
  transfers between devices with their start and end apart: 1 -> 1, of which waited for: 1 -> 1; matrix products, arithmetic and copies ran while one was open for 1% -> 2% of each run, Pallas kernels for 0% -> 0%
where the time goes in v3:
time: 183 us
  Pallas kernels  117 us (64%)
  waiting for transfers between devices  46 us (25%)
  local copies, waits for them, and re-layouts  10.4 us (6%)
  starting transfers between devices  7.3 us (4%)
    pallas_call x1, Pallas kernels, per_device(): pl.pallas_call(functools.partial(exchange_kernel, rows, wide_count, narro...  110 us
    all_to_all x1, waiting for transfers between devices, per_device(): lax.all_to_all(outgoing, ('gx', 'gy'), split_axis=0, concat_axis=0, tiled...  46 us
    unnamed x14, local copies, waits for them, and re-layouts  8.7 us
    all_to_all x1, starting transfers between devices, per_device(): lax.all_to_all(outgoing, ('gx', 'gy'), split_axis=0, concat_axis=0, tiled...  7.3 us
  transfers between devices with their start and end apart: 1, of which 1 were waited for; matrix products, arithmetic and copies ran while one was open for 2% of the time, Pallas kernels for 0%

profile of v3, /device:TPU:0, one launch (start us, length us, event | category | flops | bytes accessed | tf_op | source)
XLA Modules:
  0.0 182.7 jit_solution(4630921944127994864)
XLA Ops:
  0.0 0.8 reshape.161
  0.8 0.2 convert_reduce_fusion.1
  1.0 0.1 select_reduce_fusion.2.index_ref
  1.1 1.1 copy-done.4
  2.2 1.0 pack.1
  3.2 1.3 copy-done.2
  4.5 7.3 %all-to-all-start = ((bf16[64,128,128]{2,1,0:T(8,128)(2,1)}), bf16[64,128,128]{2,1,0:T(8,128)(2,1)S(1)}, u32[]{:S(2)}, u32[]{:S(2)}) async-start(bf16[64,128,128]{2,1,0:T(8,128)(2,1)} %copy-done.2), calls=%async_computation | async-start | bytes 4194304 | tf_op jit(solution)/shard_map/all_to_all | solution.py:268
  11.9 0.1 add.168
  12.0 0.7 broadcast_remainder_fusion
  12.7 0.1 ne.130
  12.8 0.1 ne.127
  13.2 0.1 add.173
  13.4 0.2 convert_reduce_fusion
  13.6 0.1 copy.12
  13.7 0.1 sub.61.place_ref
  13.8 0.1 select_reduce_fusion
  14.0 0.6 copy.39
  14.7 46.0 %all-to-all-done.received_ref = bf16[64,128,128]{2,1,0:T(8,128)(2,1)S(1)} async-done(((bf16[64,128,128]{2,1,0:T(8,128)(2,1)}), bf16[64,128,128]{2,1,0:T(8,128)(2,1)S(1)}, u32[]{:S(2)}, u32[]{:S(2)}) %all-to-all-start) | async-done | bytes 2097184 | tf_op jit(solution)/shard_map/all_to_all | solution.py:268
  60.7 1.5 copy-done.3
  62.3 3.5 %admit.1.own_ref = bf16[9,384,384]{2,1,0:T(8,128)(2,1)S(1)} custom-call(s32[64]{0:T(128)S(1)} %sub.61.place_ref, s32[3,27]{1,0:T(4,128)S(1)} %broadcast_add_fusion.1.inverse_ref, bf16[64,128,128]{2,1,0:T(8,128)(2,1)S(1)} %all-to-all-done.received_ref, bf16[60,128,128]{2,1,0:T(8,128)(2,1)S(1)} %bitcast.48), custom_call_target="tpu_custom_call" | custom-call | tf_op jit(solution)/shard_map/admit/pallas_call | solution.py:269
  65.7 1.5 copy-done.1
  67.2 109.9 %exchange.1.dense_ref = f32[81,128,128]{2,1,0:T(8,128)} custom-call(bf16[9,384,384]{2,1,0:T(8,128)(2,1)} %copy-done.1, f32[3,3456]{1,0:T(4,128)} %bitcast.49), custom_call_target="tpu_custom_call" | custom-call | tf_op jit(solution)/shard_map/exchange/pallas_call | solution.py:280
  177.2 2.5 %copy-done = f32[81,128,128]{2,1,0:T(8,128)S(1)} copy-done((f32[81,128,128]{2,1,0:T(8,128)S(1)}, f32[81,128,128]{2,1,0:T(8,128)}, u32[]{:S(2)}) %copy-start) | copy-done | bytes 5308440
  179.7 3.0 %pick.1 = f32[60,128,128]{2,1,0:T(8,128)} custom-call(s32[60]{0:T(128)S(1)} %multiply_add_fusion.index_ref, f32[81,128,128]{2,1,0:T(8,128)S(1)} %copy-done), custom_call_target="tpu_custom_call" | custom-call | tf_op jit(solution)/shard_map/pick/pallas_call | solution.py:301
  (28 shorter events, 0.7 us)
Async XLA Ops:
  1.1 1.1 copy-start.4
  3.2 1.3 copy-start.2
  4.5 8.7 %copy-start.5 = (s32[768]{0:T(1024)S(1)}, s32[768]{0:T(1024)}, u32[]{:S(2)}) copy-start(s32[768]{0:T(1024)} %param.9) | copy-start | bytes 9220
  4.5 56.2 %all-to-all-start = ((bf16[64,128,128]{2,1,0:T(8,128)(2,1)}), bf16[64,128,128]{2,1,0:T(8,128)(2,1)S(1)}, u32[]{:S(2)}, u32[]{:S(2)}) async-start(bf16[64,128,128]{2,1,0:T(8,128)(2,1)} %copy-done.2), calls=%async_computation | async-start | bytes 4194304 | tf_op jit(solution)/shard_map/all_to_all | solution.py:268
  60.7 1.5 copy-start.3
  65.7 1.5 copy-start.1
  177.2 2.5 %copy-start = (f32[81,128,128]{2,1,0:T(8,128)S(1)}, f32[81,128,128]{2,1,0:T(8,128)}, u32[]{:S(2)}) copy-start(f32[81,128,128]{2,1,0:T(8,128)} %exchange.1.dense_ref) | copy-start | bytes 15925252

commit v4 on v3

--- a/solution.py
+++ b/solution.py
@@ -156,7 +156,7 @@
         for edge in edges[j]:
             forward(edge)
 
-    for j in range(4):
+    for j in range(len(pairs)):
         turn(j)
     for copy in local:
         copy.wait()
@@ -164,8 +164,6 @@
         copy.wait_recv()
     for c in range(9):
         square[c] = product(left, c, 1)
-        if c in (1, 5):
-            turn(4 + c // 4)
     for copy in corners:
         copy.wait_recv()
 
@@ -188,7 +186,7 @@
         total = 3.0 * square[c] - 2.0 * total
         for r in range(rows):
             for q in range(rows):
-                out_ref[(c * rows + q) * rows + r] = total[
+                out_ref[(r * 9 + c) * rows + q] = total[
                     r * width : (r + 1) * width, q * width : (q + 1) * width
                 ]
     for copy in sides + corners:
@@ -196,8 +194,10 @@
 
 
 def pick_kernel(index_ref, dense_ref, out_ref):
+    row = pl.program_id(0)
+
     def body(i, carry):
-        out_ref[i] = dense_ref[index_ref[i]]
+        out_ref[i] = dense_ref[index_ref[row, i]]
         return carry
 
     lax.fori_loop(0, out_ref.shape[0], body, 0)
@@ -296,16 +296,15 @@
         ),
         name="exchange",
     )(own, mask)
-    row_ids = jnp.arange(rows, dtype=jnp.int32)
-    index = (spot * rows + row_ids[:, None]).reshape(-1).astype(jnp.int32)
     purified = pl.pallas_call(
         pick_kernel,
+        grid=(rows,),
         out_shape=jax.ShapeDtypeStruct((rows * slots, width, width), jnp.float32),
-        in_specs=[in_smem(), in_vmem()],
-        out_specs=in_vmem(),
+        in_specs=[in_smem(), pl.BlockSpec((9 * rows, width, width), lambda r: (r, 0, 0))],
+        out_specs=pl.BlockSpec((slots, width, width), lambda r: (r, 0, 0)),
         compiler_params=pltpu.CompilerParams(vmem_limit_bytes=32 * MIB),
         name="pick",
-    )(index, dense)
+    )(spot.astype(jnp.int32), dense)
     return purified.reshape(density.shape)
 
 

time: 183 us -> 183 us (level)
  transfers between devices with their start and end apart: 1 -> 1, of which waited for: 1 -> 1; matrix products, arithmetic and copies ran while one was open for 2% -> 1% of each run, Pallas kernels for 0% -> 0%
where the time goes in v4:
time: 183 us
  Pallas kernels  117 us (64%)
  waiting for transfers between devices  46.6 us (25%)
  local copies, waits for them, and re-layouts  9.9 us (5%)
  starting transfers between devices  7.3 us (4%)
    pallas_call x1, Pallas kernels, per_device(): pl.pallas_call(functools.partial(exchange_kernel, rows, wide_count, narro...  110 us
    all_to_all x1, waiting for transfers between devices, per_device(): lax.all_to_all(outgoing, ('gx', 'gy'), split_axis=0, concat_axis=0, tiled...  46.6 us
    unnamed x14, local copies, waits for them, and re-layouts  8.7 us
    all_to_all x1, starting transfers between devices, per_device(): lax.all_to_all(outgoing, ('gx', 'gy'), split_axis=0, concat_axis=0, tiled...  7.3 us
  transfers between devices with their start and end apart: 1, of which 1 were waited for; matrix products, arithmetic and copies ran while one was open for 1% of the time, Pallas kernels for 0%

profile of v4, /device:TPU:0, one launch (start us, length us, event | category | flops | bytes accessed | tf_op | source)
XLA Modules:
  0.0 182.8 jit_solution(10457189716713284173)
XLA Ops:
  0.0 0.8 reshape.145
  0.8 0.2 convert_reduce_fusion.1
  1.0 0.1 select_reduce_fusion.2.index_ref
  1.1 1.1 copy-done.4
  2.2 1.0 pack.1
  3.2 1.3 copy-done.2
  4.5 7.3 %all-to-all-start = ((bf16[64,128,128]{2,1,0:T(8,128)(2,1)}), bf16[64,128,128]{2,1,0:T(8,128)(2,1)S(1)}, u32[]{:S(2)}, u32[]{:S(2)}) async-start(bf16[64,128,128]{2,1,0:T(8,128)(2,1)} %copy-done.2), calls=%async_computation | async-start | bytes 4194304 | tf_op jit(solution)/shard_map/all_to_all | solution.py:268
  11.8 0.1 copy.10
  11.9 0.1 add.129
  12.0 0.1 copy.11
  12.1 0.2 convert_reduce_fusion
  12.3 0.1 copy.12
  12.4 0.1 sub.47.place_ref
  12.5 0.7 sign_compare_fusion
  13.3 0.1 select_reduce_fusion
  13.4 0.1 broadcast_bitcast_fusion
  13.5 0.6 copy.39
  14.1 46.6 %all-to-all-done.received_ref = bf16[64,128,128]{2,1,0:T(8,128)(2,1)S(1)} async-done(((bf16[64,128,128]{2,1,0:T(8,128)(2,1)}), bf16[64,128,128]{2,1,0:T(8,128)(2,1)S(1)}, u32[]{:S(2)}, u32[]{:S(2)}) %all-to-all-start) | async-done | bytes 2097184 | tf_op jit(solution)/shard_map/all_to_all | solution.py:268
  60.7 1.5 copy-done.3
  62.3 3.5 %admit.1.own_ref = bf16[9,384,384]{2,1,0:T(8,128)(2,1)S(1)} custom-call(s32[64]{0:T(128)S(1)} %sub.47.place_ref, s32[3,27]{1,0:T(4,128)S(1)} %broadcast_add_fusion.1.inverse_ref, bf16[64,128,128]{2,1,0:T(8,128)(2,1)S(1)} %all-to-all-done.received_ref, bf16[60,128,128]{2,1,0:T(8,128)(2,1)S(1)} %bitcast.48), custom_call_target="tpu_custom_call" | custom-call | tf_op jit(solution)/shard_map/admit/pallas_call | solution.py:269
  65.7 1.5 copy-done.1
  67.2 109.9 %exchange.1.dense_ref = f32[81,128,128]{2,1,0:T(8,128)} custom-call(bf16[9,384,384]{2,1,0:T(8,128)(2,1)} %copy-done.1, f32[3,3456]{1,0:T(4,128)} %bitcast.49), custom_call_target="tpu_custom_call" | custom-call | tf_op jit(solution)/shard_map/exchange/pallas_call | solution.py:280
  177.1 2.5 %copy-done = f32[81,128,128]{2,1,0:T(8,128)S(1)} copy-done((f32[81,128,128]{2,1,0:T(8,128)S(1)}, f32[81,128,128]{2,1,0:T(8,128)}, u32[]{:S(2)}) %copy-start) | copy-done | bytes 5308440
  179.6 3.1 %pick.1 = f32[60,128,128]{2,1,0:T(8,128)} custom-call(s32[3,20]{1,0:T(4,128)S(1)} %fusion.7.index_ref, f32[81,128,128]{2,1,0:T(8,128)S(1)} %copy-done), custom_call_target="tpu_custom_call" | custom-call | tf_op jit(solution)/shard_map/pick/pallas_call | solution.py:299
  (20 shorter events, 0.2 us)
Async XLA Ops:
  1.1 1.1 copy-start.4
  3.2 1.3 copy-start.2
  4.5 7.4 %copy-start.5 = (s32[768]{0:T(1024)S(1)}, s32[768]{0:T(1024)}, u32[]{:S(2)}) copy-start(s32[768]{0:T(1024)} %param.9) | copy-start | bytes 9220
  4.5 56.2 %all-to-all-start = ((bf16[64,128,128]{2,1,0:T(8,128)(2,1)}), bf16[64,128,128]{2,1,0:T(8,128)(2,1)S(1)}, u32[]{:S(2)}, u32[]{:S(2)}) async-start(bf16[64,128,128]{2,1,0:T(8,128)(2,1)} %copy-done.2), calls=%async_computation | async-start | bytes 4194304 | tf_op jit(solution)/shard_map/all_to_all | solution.py:268
  60.7 1.5 copy-start.3
  65.7 1.5 copy-start.1
  177.1 2.5 %copy-start = (f32[81,128,128]{2,1,0:T(8,128)S(1)}, f32[81,128,128]{2,1,0:T(8,128)}, u32[]{:S(2)}) copy-start(f32[81,128,128]{2,1,0:T(8,128)} %exchange.1.dense_ref) | copy-start | bytes 15925252
